TPU v7x, 32 devices: a whole 2x2x4 slice. The times are simulated.
32 devices in a mesh: groups: 2 (over y), path: 16 (over z, x, core).
Axes of the slice: x: 2, y: 2, z: 4, core: 2. Of those that a mesh axis runs over, the one named last changes fastest.
Arguments:
- tile_values: bfloat16 [1024, 9, 128, 128], P(('groups', 'path')), parts along dimension 0, may hold values from 0 to 0.0017318726
- link_of_tile: int32 [1024, 9], P(('groups', 'path')), parts along dimension 0, may hold values from 0 to 31, as said below
- tile_count: int32 [1024], P(('groups', 'path')), parts along dimension 0, may hold values from 1 to 9, as said below
- fail_links: int32 [128, 128], P('groups'), parts along dimension 0, may hold values from 0 to 4095
- flow_start: float32 [1024, 64, 128], P(('groups', 'path')), parts along dimension 0, may hold values from 0 to 1
- dual_start: float32 [64, 64, 128], P(('groups', 'path')), parts along dimension 0, may hold values from 0 to 2
- path_cost: float32 [1024, 128], P(('groups', 'path')), parts along dimension 0, may hold values from -1.5 to 0.5
- path_upper: float32 [1024, 128], P(('groups', 'path')), parts along dimension 0, may hold values from 0.5 to 2
- link_capacity: float32 [64, 128], P(('groups', 'path')), parts along dimension 0, may hold values from 2 to 8
Outputs:
- flow_final: float32 [1024, 64, 128], P(('groups', 'path')), parts along dimension 0
- dual_final: float32 [64, 64, 128], P(('groups', 'path')), parts along dimension 0
- reduced_cost: float32 [1024, 64, 128], P(('groups', 'path')), parts along dimension 0
There are 2 independent parts, one for each index of `groups`. A program takes and returns all parts, laid end to end along the dimension named above; each array names one. Nothing has to cross between parts.
Inputs may be any that keep to these rules, and one draw needn't show every extreme that they name: `link_of_tile`: the slots of one path block name link blocks of different owners (owner = link block // 2); among all slots of the 32 consecutive path blocks of one device, those reaching one owner name one and the same link block of it. `tile_count`: slots 0 to count - 1 of a path block hold its tiles. Among each 32 consecutive path blocks at least one has 9. `fail_links`: repeats are allowed.
All inputs are finite; a program needn't handle non-finite values.
Results may differ from a plain program's by a relative error of at most 0.0003.
Values may be sent and summed in bfloat16 or wider, within the bound.
A program may use at most 128 MiB of HBM per device.

v0:
```python
import jax
import jax.numpy as jnp
from jax import lax
from jax.sharding import PartitionSpec as P

ITERS = 2


primal_step = 0.5
dual_step = 0.25


def body(
    tile_values,
    link_of_tile,
    tile_count,
    fail_links,
    flow_start,
    dual_start,
    path_cost,
    path_upper,
    link_capacity,
):
    owner_total = lax.axis_size("path")
    my_index = lax.axis_index("path")
    blocks_here, slot_count, tile_width, _ = tile_values.shape
    scen_count = flow_start.shape[1]
    link_here = dual_start.shape[0]
    links_local = link_here * tile_width
    in_use = (jnp.arange(slot_count, dtype=jnp.int32)[None, :] < tile_count[:, None]).astype(
        jnp.float32
    )
    use_narrow = in_use.astype(jnp.bfloat16)
    local_ids = fail_links - my_index * links_local
    inside = (local_ids >= 0) & (local_ids < links_local)
    local_ids = jnp.where(inside, local_ids, links_local)
    scenario_ids = jnp.broadcast_to(
        jnp.arange(scen_count, dtype=jnp.int32)[:, None], fail_links.shape
    )
    surviving = (
        jnp.ones((links_local, scen_count), jnp.float32)
        .at[local_ids, scenario_ids]
        .set(0.0, mode="drop")
    )
    surviving = surviving.reshape(link_here, tile_width, scen_count).transpose(0, 2, 1)
    bound_load = link_capacity[:, None, :] * surviving

    def dual_pieces(dual_b):
        whole = lax.all_gather(dual_b, "path", axis=0, tiled=True)
        return whole[link_of_tile]

    def backward(dual_now):
        picked = dual_pieces(dual_now.astype(jnp.bfloat16)) * use_narrow[:, :, None, None]
        return jnp.einsum("bksl,bkpl->bsp", picked, tile_values, preferred_element_type=jnp.float32)

    flow_now = flow_start
    dual_now = dual_start
    cost_wide = path_cost[:, None, :]
    upper_wide = path_upper[:, None, :]
    for step in range(ITERS):
        path_push = backward(dual_now)
        new_flow = jnp.clip(flow_now - primal_step * (cost_wide + path_push), 0.0, upper_wide)
        flow_bar = (2.0 * new_flow - flow_now).astype(jnp.bfloat16)
        forward_contrib = jnp.einsum(
            "bsp,bkpl->bksl", flow_bar, tile_values, preferred_element_type=jnp.float32
        )
        partial_load = jax.ops.segment_sum(
            (forward_contrib * in_use[:, :, None, None]).reshape(-1, scen_count, tile_width),
            link_of_tile.reshape(-1),
            num_segments=owner_total * link_here,
        )
        link_load = lax.psum_scatter(partial_load, "path", scatter_dimension=0, tiled=True)
        dual_now = jnp.maximum(0.0, dual_now + dual_step * (link_load - bound_load))
        flow_now = new_flow
    reduced_cost = cost_wide + backward(dual_now)
    return (flow_now, dual_now, reduced_cost)


def solution(mesh):
    in_specs = (
        P(("groups", "path"), None, None, None),
        P(("groups", "path"), None),
        P(("groups", "path")),
        P("groups", None),
        P(("groups", "path"), None, None),
        P(("groups", "path"), None, None),
        P(("groups", "path"), None),
        P(("groups", "path"), None),
        P(("groups", "path"), None),
    )
    out_specs = (
        P(("groups", "path"), None, None),
        P(("groups", "path"), None, None),
        P(("groups", "path"), None, None),
    )
    return jax.shard_map(body, mesh=mesh, in_specs=in_specs, out_specs=out_specs, check_vma=False)
```

profile of v0, /device:TPU:0, one launch (start us, length us, event | category | flops | bytes accessed | tf_op | source)
XLA Modules:
  0.0 343.6 jit_solution(6901096730260087167)
XLA Ops:
  7.2 0.0 copy-start.2
  7.2 0.0 copy-start.11
  7.2 0.0 copy-start.10
  7.2 0.0 reduce-scatter.3.cloned.1.call-start
  7.2 0.8 compare_select_fusion.1
  8.0 0.8 copy.16
  8.8 0.7 fusion.61
  9.5 0.1 copy.15
  9.6 0.1 reshape.79
  9.7 0.8 convert_element_type.32
  10.6 24.6 %all_gather.9 = bf16[32,64,128]{2,1,0:T(8,128)(2,1)S(1)} all-gather(bf16[2,64,128]{2,1,0:T(8,128)(2,1)S(1)} %convert_element_type.32), channel_id=1, replica_groups=mesh['groups'=2,'path'=16] {'path'}, dimensions={0}, use_global_device_ids=true | all-gather | bytes 557056 | tf_op jit(solution)/shard_map/all_gather | solution.py:49
  35.1 0.1 reshape.103
  35.2 13.3 %gather_fusion = bf16[288,64,128]{2,1,0:T(8,128)(2,1)} fusion(bf16[32,64,128]{2,1,0:T(8,128)(2,1)S(1)} %all_gather.9, s32[1024]{0:T(1024)S(1)} %pad_clamp_fusion), kind=kCustom, calls=%fused_computation | custom fusion | bytes 9438336 | tf_op jit(solution)/shard_map/gather | solution.py:50
  48.6 0.0 copy-done.2
  48.6 0.0 copy-done.11
  48.6 0.0 copy-done.10
  48.6 8.8 %fusion.45 = f32[32,64,128]{2,1,0:T(8,128)S(1)} fusion(f32[32,64,128]{2,1,0:T(8,128)S(1)} %copy-done.2, bf16[32,9,128,128]{3,2,1,0:T(8,128)(2,1)} %param.9, bf16[32,9,64,128]{3,2,1,0:T(8,128)(2,1)} %bitcast.92, bf16[32,9]{1,0:T(8,128)(2,1)S(1)} %get-tuple-element.6, f32[32,128]{1,0:T(8,128)S(1)} %copy-done.11, f32[32,128]{1,0:T(8,128)S(1)} %copy-done.10), kind=kOutput, calls=%fused_computation.29 | convolution fusion | flops 607649792 | bytes 16286272 | tf_op jit(solution)/shard_map/bksl,bkpl->bsp/dot_general | solution.py:54
  57.4 8.8 %broadcast_multiply_fusion.1 = f32[32,64,9,128]{3,1,2,0:T(8,128)} fusion(f32[32,9]{1,0:T(8,128)S(1)} %get-tuple-element.5, bf16[32,9,128,128]{3,2,1,0:T(8,128)(2,1)} %param.9, f32[32,64,128]{2,1,0:T(8,128)S(1)} %copy-done.2, f32[32,64,128]{2,1,0:T(8,128)S(1)} %fusion.45), kind=kOutput, calls=%fused_computation.11 | convolution fusion | flops 607125504 | bytes 20972672 | tf_op jit(solution)/shard_map/bsp,bkpl->bksl/dot_general | solution.py:64
  66.3 0.1 max.18.clone
  66.4 0.0 copy-start.6
  66.4 0.0 copy-start.9
  66.4 0.0 copy-start.8
  66.4 0.0 copy-start.4
  66.4 0.0 copy-start.7
  66.4 29.8 %scatter_fusion = f32[32,64,128]{2,1,0:T(8,128)S(1)} fusion(f32[32,64,128]{2,1,0:T(8,128)S(1)} %max.18.clone, s32[288]{0:T(512)S(1)} %reshape.103, f32[288,64,128]{2,1,0:T(8,128)} %bitcast.90), kind=kCustom, calls=%fused_computation.3 | custom fusion | flops 2359296 | bytes 28312704 | tf_op jit(solution)/shard_map/scatter-add | solution.py:67
  96.3 0.0 copy-start.1
  96.3 1.0 copy-done.1
  97.2 0.0 reduce-scatter.3.cloned.1.call-update
  97.3 0.0 reduce-scatter.5.cloned.1.call-start
  97.3 0.0 copy-done.6
  97.4 0.0 copy-done.9
  97.4 0.1 multiply_reduce_fusion
  97.4 0.0 copy-done.8
  97.4 0.1 and_reduce_fusion
  97.6 30.5 %scatter_custom_fusion.2 = f32[16384]{0:T(1024)S(1)} fusion(s32[8192]{0:T(1024)S(1)} %select_bitcast_fusion, f32[8192]{0:T(1024)S(1)} %broadcast.96, f32[]{:T(128)} %constant.14.clone.1), kind=kCustom, calls=%fused_computation.46 | custom fusion | bytes 65540
  128.1 24.1 %reduce-scatter.3.cloned.1.call-done = f32[2,64,128]{2,1,0:T(8,128)} async-done(((f32[32,64,128]{2,1,0:T(8,128)}), f32[2,64,128]{2,1,0:T(8,128)}) %reduce-scatter.3.cloned.1.call-update) | async-done | bytes 65552 | tf_op jit(solution)/shard_map/reduce_scatter | solution.py:72
  152.1 0.0 copy-done.4
  152.1 0.0 copy-done.7
  152.1 0.9 fusion.62
  153.0 21.0 %all_gather.10 = bf16[32,64,128]{2,1,0:T(8,128)(2,1)S(1)} all-gather(bf16[2,64,128]{2,1,0:T(8,128)(2,1)S(1)} %fusion.62), channel_id=1, replica_groups=mesh['groups'=2,'path'=16] {'path'}, dimensions={0}, use_global_device_ids=true | all-gather | bytes 557056 | tf_op jit(solution)/shard_map/all_gather | solution.py:49
  174.0 13.3 %gather_fusion.1 = bf16[288,64,128]{2,1,0:T(8,128)(2,1)} fusion(bf16[32,64,128]{2,1,0:T(8,128)(2,1)S(1)} %all_gather.10, s32[1024]{0:T(1024)S(1)} %pad_clamp_fusion), kind=kCustom, calls=%fused_computation.1 | custom fusion | bytes 9438336 | tf_op jit(solution)/shard_map/gather | solution.py:50
  187.4 8.8 %fusion.48 = f32[32,64,128]{2,1,0:T(8,128)S(1)} fusion(f32[32,64,128]{2,1,0:T(8,128)S(1)} %fusion.45, bf16[32,9,128,128]{3,2,1,0:T(8,128)(2,1)} %param.9, bf16[32,9,64,128]{3,2,1,0:T(8,128)(2,1)} %bitcast.93, bf16[32,9]{1,0:T(8,128)(2,1)S(1)} %get-tuple-element.6, f32[32,128]{1,0:T(8,128)S(1)} %copy-done.11, f32[32,128]{1,0:T(8,128)S(1)} %copy-done.10), kind=kOutput, calls=%fused_computation.30 | convolution fusion | flops 607649792 | bytes 16286272 | tf_op jit(solution)/shard_map/bksl,bkpl->bsp/dot_general | solution.py:54
  196.2 0.0 copy-start.3
  196.2 9.2 %broadcast_multiply_fusion = f32[32,64,9,128]{3,1,2,0:T(8,128)} fusion(f32[32,9]{1,0:T(8,128)S(1)} %get-tuple-element.5, bf16[32,9,128,128]{3,2,1,0:T(8,128)(2,1)} %param.9, f32[32,64,128]{2,1,0:T(8,128)S(1)} %fusion.45, f32[32,64,128]{2,1,0:T(8,128)S(1)} %fusion.48), kind=kOutput, calls=%fused_computation.10 | convolution fusion | flops 607125504 | bytes 20972672 | tf_op jit(solution)/shard_map/bsp,bkpl->bksl/dot_general | solution.py:64
  205.4 0.0 copy-done.3
  205.4 0.1 max.18
  205.5 0.0 copy-start.5
  205.5 29.8 %scatter_fusion.1 = f32[32,64,128]{2,1,0:T(8,128)S(1)} fusion(f32[32,64,128]{2,1,0:T(8,128)S(1)} %max.18, s32[288]{0:T(512)S(1)} %reshape.103, f32[288,64,128]{2,1,0:T(8,128)} %bitcast.89), kind=kCustom, calls=%fused_computation.4 | custom fusion | flops 2359296 | bytes 28312704 | tf_op jit(solution)/shard_map/scatter-add | solution.py:67
  235.4 0.0 copy-start
  235.4 1.0 copy-done
  236.3 0.0 reduce-scatter.5.cloned.1.call-update
  236.4 54.8 %reduce-scatter.5.cloned.1.call-done = f32[2,64,128]{2,1,0:T(8,128)} async-done(((f32[32,64,128]{2,1,0:T(8,128)}), f32[2,64,128]{2,1,0:T(8,128)}) %reduce-scatter.5.cloned.1.call-update) | async-done | bytes 65552 | tf_op jit(solution)/shard_map/reduce_scatter | solution.py:72
  291.2 0.0 copy-done.5
  291.2 1.5 fusion.66
  292.7 21.0 %all_gather.11 = bf16[32,64,128]{2,1,0:T(8,128)(2,1)S(1)} all-gather(bf16[2,64,128]{2,1,0:T(8,128)(2,1)S(1)} %get-tuple-element.3), channel_id=1, replica_groups=mesh['groups'=2,'path'=16] {'path'}, dimensions={0}, use_global_device_ids=true | all-gather | bytes 557056 | tf_op jit(solution)/shard_map/all_gather | solution.py:49
  313.7 13.3 %gather_fusion.2 = bf16[288,64,128]{2,1,0:T(8,128)(2,1)} fusion(bf16[32,64,128]{2,1,0:T(8,128)(2,1)S(1)} %all_gather.11, s32[1024]{0:T(1024)S(1)} %pad_clamp_fusion), kind=kCustom, calls=%fused_computation.2 | custom fusion | bytes 9438336 | tf_op jit(solution)/shard_map/gather | solution.py:50
  327.0 9.8 %fusion.18 = f32[32,64,128]{2,1,0:T(8,128)} fusion(bf16[32,9,128,128]{3,2,1,0:T(8,128)(2,1)} %param.9, bf16[32,9,64,128]{3,2,1,0:T(8,128)(2,1)} %bitcast.91, bf16[32,9]{1,0:T(8,128)(2,1)S(1)} %get-tuple-element.6, f32[32,128]{1,0:T(8,128)S(1)} %copy-done.11), kind=kOutput, calls=%fused_computation.20 | convolution fusion | flops 606601216 | bytes 15221312 | tf_op jit(solution)/shard_map/bksl,bkpl->bsp/dot_general | solution.py:54
  (6 shorter events, 0.1 us)
Async XLA Ops:
  7.2 41.4 %copy-start.2 = (f32[32,64,128]{2,1,0:T(8,128)S(1)}, f32[32,64,128]{2,1,0:T(8,128)}, u32[]{:S(2)}) copy-start(f32[32,64,128]{2,1,0:T(8,128)} %param.13) | copy-start | bytes 3145732
  7.2 41.4 %copy-start.11 = (f32[32,128]{1,0:T(8,128)S(1)}, f32[32,128]{1,0:T(8,128)}, u32[]{:S(2)}) copy-start(f32[32,128]{1,0:T(8,128)} %param.15) | copy-start | bytes 49156
  7.2 41.4 %copy-start.10 = (f32[32,128]{1,0:T(8,128)S(1)}, f32[32,128]{1,0:T(8,128)}, u32[]{:S(2)}) copy-start(f32[32,128]{1,0:T(8,128)} %param.16) | copy-start | bytes 49156
  7.2 144.9 %reduce-scatter.3.cloned.1.call-start = ((), (), s32[]{:S(2)}) async-start(), calls=%async_computation.2 | async-start | bytes 1114112 | tf_op jit(solution)/shard_map/reduce_scatter | solution.py:72
  66.4 30.9 %copy-start.6 = (s32[64,128]{1,0:T(8,128)S(1)}, s32[64,128]{1,0:T(8,128)}, u32[]{:S(2)}) copy-start(s32[64,128]{1,0:T(8,128)} %param.12) | copy-start | bytes 98308
  66.4 31.0 %copy-start.9 = (s32[2]{0:T(128)S(1)}, s32[2]{0:T(128)}, u32[]{:S(2)}) copy-start(s32[2]{0:T(128)} %constant.6) | copy-start | bytes 28
  66.4 31.0 %copy-start.8 = (s32[2]{0:T(128)S(1)}, s32[2]{0:T(128)}, u32[]{:S(2)}) copy-start(s32[2]{0:T(128)} %constant.32) | copy-start | bytes 28
  66.4 85.7 %copy-start.4 = (f32[2,64,128]{2,1,0:T(8,128)S(1)}, f32[2,64,128]{2,1,0:T(8,128)}, u32[]{:S(2)}) copy-start(f32[2,64,128]{2,1,0:T(8,128)} %param.14) | copy-start | bytes 196612
  66.4 85.7 %copy-start.7 = (f32[2,128]{1,0:T(2,128)S(1)}, f32[2,128]{1,0:T(2,128)}, u32[]{:S(2)}) copy-start(f32[2,128]{1,0:T(2,128)} %param.17) | copy-start | bytes 3076
  96.3 1.0 copy-start.1
  97.3 193.9 %reduce-scatter.5.cloned.1.call-start = ((), (), s32[]{:S(2)}) async-start(), calls=%async_computation.3 | async-start | bytes 1114112 | tf_op jit(solution)/shard_map/reduce_scatter | solution.py:72
  196.2 9.2 %copy-start.3 = (f32[32,64,128]{2,1,0:T(8,128)}, f32[32,64,128]{2,1,0:T(8,128)S(1)}, u32[]{:S(2)}) copy-start(f32[32,64,128]{2,1,0:T(8,128)S(1)} %fusion.48) | copy-start | bytes 3145732
  205.5 85.6 %copy-start.5 = (f32[2,64,128]{2,1,0:T(8,128)S(1)}, f32[2,64,128]{2,1,0:T(8,128)}, u32[]{:S(2)}) copy-start(f32[2,64,128]{2,1,0:T(8,128)} %reduce-scatter.3.cloned.1.call-done) | copy-start | bytes 196612
  235.4 1.0 copy-start
Sparse Core Ops, SparseCore 0:
  97.4 54.7 reduce-scatter.2
  236.5 54.6 reduce-scatter.4
where the time goes:
time: 346 us; the launch traced here: 344 us
  waiting for transfers between devices  78.9 us (23%)
  local copies, waits for them, and re-layouts  73.7 us (21%)
  blocking collectives  66.6 us (19%)
  other arithmetic  64.5 us (19%)
  matrix products  45.5 us (13%)
  between operations  14.3 us (4%)
    reduce_scatter x2, waiting for transfers between devices, body(): lax.psum_scatter(partial_load, 'path', scatter_dimension=0, tiled=True)  78.9 us
    all_gather x3, blocking collectives, dual_pieces(): whole = lax.all_gather(dual_b, 'path', axis=0, tiled=True)  66.6 us
    scatter-add x2, other arithmetic, body(): jax.ops.segment_sum((forward_contrib * in_use[:, :, None, None]).reshape(...  59.6 us
    gather x3, local copies, waits for them, and re-layouts, dual_pieces(): return whole[link_of_tile]  39.9 us
    unnamed x28, local copies, waits for them, and re-layouts  33.3 us
    dot_general x3, matrix products, backward(): jnp.einsum('bksl,bkpl->bsp', picked, tile_values, preferred_element_type=...  27.5 us
    dot_general x2, matrix products, body(): jnp.einsum('bsp,bkpl->bksl', flow_bar, tile_values, preferred_element_typ...  18 us
  transfers between devices with their start and end apart: 2, of which 2 were waited for; matrix products, arithmetic and copies ran while one was open for 9% of the time, Pallas kernels for 0%

commit v1 on v0

v1 whole, which is shorter than its diff:
```python
import functools

import jax
import jax.numpy as jnp
from jax import lax
from jax.experimental import pallas as pl
from jax.experimental.pallas import tpu as pltpu
from jax.sharding import PartitionSpec as P

ITERS = 2
QUAD = 4
CHUNK = 8

primal_step = 0.5
dual_step = 0.25


def mix(a, b, count):
    if count & (count - 1):
        return lax.rem(a + b, count)
    total = 0
    bit = 1
    while bit < count:
        total = total + ((a // bit + b // bit) % 2) * bit
        bit *= 2
    return total


def kernel(
    devs,
    inv_ref,
    sel_ref,
    fail_ref,
    dual_ref,
    cost_ref,
    upper_ref,
    cap_ref,
    tiles_hbm,
    flow_hbm,
    dual_out,
    flow_out,
    rc_out,
    tiles,
    flow,
    push,
    bar,
    bound,
    send_dual,
    recv_dual,
    send_part,
    recv_part,
    recv_sel,
    acc,
    tile_sem,
    flow_sem,
    out_sem,
    sel_send,
    sel_recv,
    dual_send,
    dual_recv,
    part_send,
    part_recv,
):
    me = lax.axis_index("path")
    groups = devs // QUAD
    my_group = me // QUAD
    link_here, scen, width = dual_ref.shape
    tile_total = tiles.shape[0] - 1
    blocks = flow.shape[0]
    chunks = blocks // CHUNK
    load_parts = 4
    piece = tile_total // load_parts

    def load_tiles(i):
        part = pl.ds(i * piece, piece)
        return pltpu.make_async_copy(tiles_hbm.at[part], tiles.at[part], tile_sem.at[i])

    for i in range(load_parts):
        load_tiles(i).start()
    load_flow = pltpu.make_async_copy(flow_hbm, flow, flow_sem)
    load_flow.start()

    def remote(src, dst, send, recv, peer):
        return pltpu.make_async_remote_copy(
            src_ref=src.at[peer],
            dst_ref=dst.at[me],
            send_sem=send.at[peer],
            recv_sem=recv.at[me],
            device_id={"path": peer},
            device_id_type=pl.DeviceIdType.MESH,
        )

    def arrival(src, dst, send, recv, peer):
        return pltpu.make_async_remote_copy(
            src_ref=src.at[peer],
            dst_ref=dst.at[peer],
            send_sem=send.at[peer],
            recv_sem=recv.at[peer],
            device_id={"path": peer},
            device_id_type=pl.DeviceIdType.MESH,
        )

    sel_ways = (sel_ref, recv_sel, sel_send, sel_recv)
    dual_ways = (send_dual, recv_dual, dual_send, dual_recv)
    part_ways = (send_part, recv_part, part_send, part_recv)

    def peers(step, far_first=True):
        def one(g, _):
            base = mix(my_group, groups - 1 - g if far_first else g, groups) * QUAD
            for i in range(QUAD):
                peer = base + i

                @pl.when(peer != me)
                def _():
                    step(peer)

            return 0

        lax.fori_loop(0, groups, one, 0)

    barrier = pltpu.get_barrier_semaphore()

    def greet(peer):
        pl.semaphore_signal(
            barrier, inc=1, device_id={"path": peer}, device_id_type=pl.DeviceIdType.MESH
        )

    peers(greet)
    pl.semaphore_wait(barrier, devs - 1)

    peers(lambda peer: remote(*sel_ways, peer).start())
    recv_sel[me] = sel_ref[me]

    tiles[tile_total] = jnp.zeros((width, width), tiles.dtype)
    first_link = me * (link_here * width)
    lane = lax.broadcasted_iota(jnp.int32, (scen, width), 1) + first_link
    for half in range(fail_ref.shape[1] // width):
        ids = fail_ref[:, half * width : (half + 1) * width]

        def strike(_, state):
            ids, *alive = state
            for f in range(8):
                struck = jnp.broadcast_to(ids[:, f : f + 1], (scen, width))
                alive = [
                    jnp.where(struck == lane + b * width, 0.0, alive[b]) for b in range(link_here)
                ]
            return (pltpu.roll(ids, width - 8, 1), *alive)

        if half == 0:
            alive = [jnp.ones((scen, width), jnp.float32) for _ in range(link_here)]
        _, *alive = lax.fori_loop(0, width // 8, strike, (ids, *alive))
    for b in range(link_here):
        bound[b] = cap_ref[b : b + 1, :] * alive[b]
        dual_out[b] = dual_ref[b]

    peers(lambda peer: arrival(*sel_ways, peer).wait_recv(), far_first=False)
    peers(lambda peer: arrival(*sel_ways, peer).wait_send())

    def give(dst, index, peer):
        choice = recv_sel[peer][0:1, :]
        picked = dual_out[0]
        for b in range(1, link_here):
            picked = jnp.where(choice == b, dual_out[b], picked)
        dst[index] = picked.astype(jnp.bfloat16)

    def weights(base, c, i, h):
        rows = []
        for r in range(2):
            row = [
                tiles[inv_ref[base + 2 * h + q, c * CHUNK + 2 * i + r]] for q in range(2)
            ]
            rows.append(jnp.concatenate(row, axis=1))
        return jnp.concatenate(rows, axis=0)

    def backward():
        def quad(g, _):
            base = mix(my_group, g, groups) * QUAD
            for i in range(QUAD):

                @pl.when(base + i != me)
                def _():
                    arrival(*dual_ways, base + i).wait_recv()

            def chunk(c, _):
                pairs = [
                    jnp.concatenate([recv_dual[base + 2 * h], recv_dual[base + 2 * h + 1]], axis=1)
                    for h in range(QUAD // 2)
                ]
                for i in range(CHUNK // 2):
                    total = push[c, :, 2 * i * width : 2 * (i + 1) * width]
                    for h in range(QUAD // 2):
                        total = total + lax.dot_general(
                            pairs[h],
                            weights(base, c, i, h),
                            (((1,), (1,)), ((), ())),
                            preferred_element_type=jnp.float32,
                        )
                    push[c, :, 2 * i * width : 2 * (i + 1) * width] = total
                return 0

            return lax.fori_loop(0, chunks, chunk, 0)

        push[...] = jnp.zeros(push.shape, push.dtype)
        lax.fori_loop(0, groups, quad, 0)

    def primal():
        def block(c, _):
            for i in range(CHUNK):
                b = c * CHUNK + i
                side = slice(i * width, (i + 1) * width)
                now = flow[b]
                price = cost_ref[pl.ds(b, 1), :] + push[c, :, side]
                new = jnp.clip(now - primal_step * price, 0.0, upper_ref[pl.ds(b, 1), :])
                bar[c, :, side] = (2.0 * new - now).astype(jnp.bfloat16)
                flow[b] = new
            return 0

        lax.fori_loop(0, chunks, block, 0)

    def forward():
        def quad(g, _):
            base = mix(my_group, groups - 1 - g, groups) * QUAD

            def chunk(c, _):
                for h in range(QUAD // 2):
                    total = acc[h]
                    for i in range(CHUNK // 2):
                        total = total + jnp.dot(
                            bar[c, :, 2 * i * width : 2 * (i + 1) * width],
                            weights(base, c, i, h),
                            preferred_element_type=jnp.float32,
                        )
                    acc[h] = total
                return 0

            acc[...] = jnp.zeros(acc.shape, acc.dtype)
            lax.fori_loop(0, chunks, chunk, 0)
            for i in range(QUAD):
                owner = base + i
                load = acc[i // 2, :, (i % 2) * width : (i % 2 + 1) * width]

                @pl.when(owner != me)
                def _():
                    send_part[owner] = load
                    remote(*part_ways, owner).start()

                @pl.when(owner == me)
                def _():
                    recv_part[me] = load

            return 0

        lax.fori_loop(0, groups, quad, 0)

    def dual_step_all():
        def add(g, loads):
            base = mix(my_group, groups - 1 - g, groups) * QUAD
            for i in range(QUAD):

                @pl.when(base + i != me)
                def _():
                    arrival(*part_ways, base + i).wait_recv()

            for i in range(QUAD):
                part = recv_part[base + i]
                choice = recv_sel[base + i][0:1, :]
                loads = tuple(
                    loads[b] + jnp.where(choice == b, part, 0.0) for b in range(link_here)
                )
            return loads

        zero = jnp.zeros((scen, width), jnp.float32)
        loads = lax.fori_loop(0, groups, add, (zero,) * link_here)
        for b in range(link_here):
            dual_out[b] = jnp.maximum(0.0, dual_out[b] + dual_step * (loads[b] - bound[b]))

    save_flow = pltpu.make_async_copy(flow, flow_out, flow_sem)

    def phase(t, _):
        def offer(peer):
            give(send_dual, peer, peer)
            remote(*dual_ways, peer).start()

        peers(offer)
        give(recv_dual, me, me)

        @pl.when(t == 0)
        def _():
            for i in range(load_parts):
                load_tiles(i).wait()
            load_flow.wait()

        backward()
        peers(lambda peer: arrival(*dual_ways, peer).wait_send())

        @pl.when(t < ITERS)
        def _():
            primal()

            @pl.when(t == ITERS - 1)
            def _():
                save_flow.start()

            forward()
            dual_step_all()
            peers(lambda peer: arrival(*part_ways, peer).wait_send())

        return 0

    lax.fori_loop(0, ITERS + 1, phase, 0)
    save_flow.wait()

    def finish(c, _):
        for i in range(CHUNK):
            b = c * CHUNK + i
            flow[b] = cost_ref[pl.ds(b, 1), :] + push[c, :, i * width : (i + 1) * width]
        part = pl.ds(c * CHUNK, CHUNK)
        pltpu.make_async_copy(flow.at[part], rc_out.at[part], out_sem.at[c]).start()
        return 0

    lax.fori_loop(0, chunks, finish, 0)

    def close(c, _):
        part = pl.ds(c * CHUNK, CHUNK)
        pltpu.make_async_copy(flow.at[part], rc_out.at[part], out_sem.at[c]).wait()
        return 0

    lax.fori_loop(0, chunks, close, 0)


def body(
    tile_values,
    link_of_tile,
    tile_count,
    fail_links,
    flow_start,
    dual_start,
    path_cost,
    path_upper,
    link_capacity,
):
    devs = lax.axis_size("path")
    blocks, slots, width, _ = tile_values.shape
    link_here, scen, _ = dual_start.shape
    tile_total = blocks * slots
    owner_of = link_of_tile // link_here
    used = jnp.arange(slots, dtype=jnp.int32)[None, :] < tile_count[:, None]
    hits = (owner_of[None] == jnp.arange(devs, dtype=jnp.int32)[:, None, None]) & used[None]
    place = jnp.arange(tile_total, dtype=jnp.int32).reshape(1, blocks, slots)
    inv = jnp.min(jnp.where(hits, place, tile_total), axis=2)
    sel = jnp.max(jnp.where(hits, (link_of_tile % link_here)[None], 0), axis=(1, 2))
    sel = jnp.broadcast_to(sel[:, None, None], (devs, 8, width))
    chunks = blocks // CHUNK
    vmem = pl.BlockSpec(memory_space=pltpu.VMEM)
    anywhere = pl.BlockSpec(memory_space=pl.ANY)
    dma = pltpu.SemaphoreType.DMA
    dual_final, flow_final, reduced = pl.pallas_call(
        functools.partial(kernel, devs),
        out_shape=(
            jax.ShapeDtypeStruct(dual_start.shape, jnp.float32),
            jax.ShapeDtypeStruct(flow_start.shape, jnp.float32),
            jax.ShapeDtypeStruct(flow_start.shape, jnp.float32),
        ),
        in_specs=[pl.BlockSpec(memory_space=pltpu.SMEM)] + [vmem] * 6 + [anywhere] * 2,
        out_specs=(vmem, anywhere, anywhere),
        scratch_shapes=[
            pltpu.VMEM((tile_total + 1, width, width), jnp.bfloat16),
            pltpu.VMEM(flow_start.shape, jnp.float32),
            pltpu.VMEM((chunks, scen, CHUNK * width), jnp.float32),
            pltpu.VMEM((chunks, scen, CHUNK * width), jnp.bfloat16),
            pltpu.VMEM(dual_start.shape, jnp.float32),
            pltpu.VMEM((devs, scen, width), jnp.bfloat16),
            pltpu.VMEM((devs, scen, width), jnp.bfloat16),
            pltpu.VMEM((devs, scen, width), jnp.float32),
            pltpu.VMEM((devs, scen, width), jnp.float32),
            pltpu.VMEM((devs, 8, width), jnp.int32),
            pltpu.VMEM((QUAD // 2, scen, 2 * width), jnp.float32),
            dma((4,)),
            dma(()),
            dma((chunks,)),
            dma((devs,)),
            dma((devs,)),
            dma((devs,)),
            dma((devs,)),
            dma((devs,)),
            dma((devs,)),
        ],
        compiler_params=pltpu.CompilerParams(
            collective_id=0, has_side_effects=True, vmem_limit_bytes=48 * 1024 * 1024
        ),
    )(
        inv,
        sel,
        fail_links,
        dual_start,
        path_cost,
        path_upper,
        link_capacity,
        tile_values.reshape(tile_total, width, width),
        flow_start,
    )
    return flow_final, dual_final, reduced


def solution(mesh):
    rows = ("groups", "path")
    in_specs = (
        P(rows, None, None, None),
        P(rows, None),
        P(rows),
        P("groups", None),
        P(rows, None, None),
        P(rows, None, None),
        P(rows, None),
        P(rows, None),
        P(rows, None),
    )
    out_specs = (P(rows, None, None), P(rows, None, None), P(rows, None, None))
    return jax.shard_map(body, mesh=mesh, in_specs=in_specs, out_specs=out_specs, check_vma=False)
```

time: 346 us -> 86.3 us (0.25)
  waiting for transfers between devices: 78.9 us -> 0 us
  Pallas kernels: 0 us -> 76.1 us
  blocking collectives: 66.6 us -> 0 us
  local copies, waits for them, and re-layouts: 73.7 us -> 7.58 us
  other arithmetic: 64.5 us -> 1.52 us
  matrix products: 45.5 us -> 0 us
  between operations: 14.3 us -> 0.66 us
    reduce_scatter x2 -> x0, waiting for transfers between devices: 78.9 us -> none  [body(): lax.psum_scatter(partial_load, 'path', scatter_dimension=0, tiled=True)]
    pallas_call x0 -> x1, Pallas kernels: none -> 76.1 us  [body(): pl.pallas_call(functools.partial(kernel, devs), out_shape=(jax.ShapeDtype...]
    all_gather x3 -> x0, blocking collectives: 66.6 us -> none  [dual_pieces(): whole = lax.all_gather(dual_b, 'path', axis=0, tiled=True)]
    scatter-add x2 -> x0, other arithmetic: 59.6 us -> none  [body(): jax.ops.segment_sum((forward_contrib * in_use[:, :, None, None]).reshape(...]
    dot_general x5 -> x0, matrix products: 45.5 us -> none  [the longest x3 27.5 us: backward(): jnp.einsum('bksl,bkpl->bsp', picked, tile_values, preferred_element_type=...]
    gather x3 -> x0, local copies, waits for them, and re-layouts: 39.9 us -> none  [dual_pieces(): return whole[link_of_tile]]
    unnamed x28 -> x15, local copies, waits for them, and re-layouts: 33.3 us -> 7.51 us
    convert_element_type x4 -> x0, other arithmetic: 3.93 us -> none  [the longest x3 3.21 us: backward(): dual_now.astype(jnp.bfloat16)]
  transfers between devices with their start and end apart: 2 -> 0, of which waited for: 2 -> 0; matrix products, arithmetic and copies ran while one was open for 9% -> 0% of each run, Pallas kernels for 0% -> 0%
where the time goes in v1:
time: 86.3 us; the launch traced here: 85.9 us
  Pallas kernels  76.1 us (88%)
  local copies, waits for them, and re-layouts  7.58 us (9%)
  other arithmetic  1.52 us (2%)
    pallas_call x1, Pallas kernels, body(): pl.pallas_call(functools.partial(kernel, devs), out_shape=(jax.ShapeDtype...  76.1 us
    unnamed x15, local copies, waits for them, and re-layouts  7.51 us

profile of v1, /device:TPU:0, one launch (start us, length us, event | category | flops | bytes accessed | tf_op | source)
XLA Modules:
  0.0 85.9 jit_solution(3293068173347214579)
XLA Ops:
  0.6 0.7 iota_compare_fusion.1
  1.3 0.7 add_select_fusion.1
  2.0 0.1 select_reduce_fusion
  2.1 0.1 broadcast_in_dim.36.sel_ref
  2.2 0.0 copy-start
  2.2 1.2 %copy-done = f32[32,64,128]{2,1,0:T(8,128)S(1)} copy-done((f32[32,64,128]{2,1,0:T(8,128)S(1)}, f32[32,64,128]{2,1,0:T(8,128)}, u32[]{:S(2)}) %copy-start) | copy-done | bytes 1048600
  3.5 0.0 copy-start.1
  3.5 0.8 copy-done.1
  4.3 0.0 copy-start.2
  4.3 0.8 copy-done.2
  5.1 0.0 copy-start.3
  5.1 0.7 copy-done.3
  5.8 0.0 copy-start.4
  5.8 0.7 copy-done.4
  6.5 0.0 copy-start.5
  6.5 0.7 copy-done.5
  7.2 76.1 %shard_map.112 = (f32[2,64,128]{2,1,0:T(8,128)S(1)}, f32[32,64,128]{2,1,0:T(8,128)S(1)}, f32[32,64,128]{2,1,0:T(8,128)S(1)}) custom-call(s32[16,32]{1,0:T(8,128)S(1)} %get-tuple-element.10.inv_ref, s32[16,8,128]{2,1,0:T(8,128)S(1)} %broadcast_in_dim.36.sel_ref, s32[64,128]{1,0:T(8,128)S(1)} %copy-done.2, f32[2,64,128]{2,1,0:T(8,128)S(1)} %copy-done.1, ...), custom_call_target="tpu_custom_call" | custom-call | tf_op jit(solution)/shard_map/pallas_call | solution.py:357
  83.3 1.0 %copy.17 = f32[32,64,128]{2,1,0:T(8,128)} copy(f32[32,64,128]{2,1,0:T(8,128)S(1)} %get-tuple-element.17) | data formatting | bytes 2097152
  84.3 0.6 copy.18
  84.9 1.0 %copy.19 = f32[32,64,128]{2,1,0:T(8,128)} copy(f32[32,64,128]{2,1,0:T(8,128)S(1)} %get-tuple-element.19) | data formatting | bytes 2097152
Async XLA Ops:
  2.2 1.2 %copy-start = (f32[32,64,128]{2,1,0:T(8,128)S(1)}, f32[32,64,128]{2,1,0:T(8,128)}, u32[]{:S(2)}) copy-start(f32[32,64,128]{2,1,0:T(8,128)} %flow_hbm.1) | copy-start | bytes 3145732
  3.5 0.8 copy-start.1
  4.3 0.8 copy-start.2
  5.1 0.7 copy-start.3
  5.8 0.7 copy-start.4
  6.5 0.7 copy-start.5

commit v2 on v1

--- a/solution.py
+++ b/solution.py
@@ -9,7 +9,9 @@
 
 ITERS = 2
 QUAD = 4
-CHUNK = 8
+CHUNK = 32
+LEVELS = 32000.0
+PIECES = 4
 
 primal_step = 0.5
 dual_step = 0.25
@@ -28,6 +30,18 @@
 
 def kernel(
     devs,
+    inv_hbm,
+    sel_hbm,
+    fail_hbm,
+    dual_hbm,
+    cost_hbm,
+    upper_hbm,
+    cap_hbm,
+    tiles_hbm,
+    flow_hbm,
+    dual_out,
+    flow_out,
+    rc_out,
     inv_ref,
     sel_ref,
     fail_ref,
@@ -35,12 +49,9 @@
     cost_ref,
     upper_ref,
     cap_ref,
-    tiles_hbm,
-    flow_hbm,
-    dual_out,
-    flow_out,
-    rc_out,
+    small_sem,
     tiles,
+    turned,
     flow,
     push,
     bar,
@@ -50,7 +61,6 @@
     send_part,
     recv_part,
     recv_sel,
-    acc,
     tile_sem,
     flow_sem,
     out_sem,
@@ -75,6 +85,22 @@
         part = pl.ds(i * piece, piece)
         return pltpu.make_async_copy(tiles_hbm.at[part], tiles.at[part], tile_sem.at[i])
 
+    small = [
+        pltpu.make_async_copy(src, dst, small_sem.at[i])
+        for i, (src, dst) in enumerate(
+            (
+                (sel_hbm, sel_ref),
+                (dual_hbm, dual_ref),
+                (fail_hbm, fail_ref),
+                (cap_hbm, cap_ref),
+                (inv_hbm, inv_ref),
+                (cost_hbm, cost_ref),
+                (upper_hbm, upper_ref),
+            )
+        )
+    ]
+    for copy in small:
+        copy.start()
     for i in range(load_parts):
         load_tiles(i).start()
     load_flow = pltpu.make_async_copy(flow_hbm, flow, flow_sem)
@@ -126,12 +152,15 @@
         )
 
     peers(greet)
+    for copy in small:
+        copy.wait()
     pl.semaphore_wait(barrier, devs - 1)
 
     peers(lambda peer: remote(*sel_ways, peer).start())
     recv_sel[me] = sel_ref[me]
 
     tiles[tile_total] = jnp.zeros((width, width), tiles.dtype)
+    turned[tile_total] = jnp.zeros((width, width), tiles.dtype)
     first_link = me * (link_here * width)
     lane = lax.broadcasted_iota(jnp.int32, (scen, width), 1) + first_link
     for half in range(fail_ref.shape[1] // width):
@@ -172,6 +201,20 @@
             rows.append(jnp.concatenate(row, axis=1))
         return jnp.concatenate(rows, axis=0)
 
+    def weights_turned(base, c, i, h):
+        rows = []
+        for q in range(2):
+            row = [
+                turned[inv_ref[base + 2 * h + q, c * CHUNK + 2 * i + r]] for r in range(2)
+            ]
+            rows.append(jnp.concatenate(row, axis=1))
+        return jnp.concatenate(rows, axis=0)
+
+    def turn(k, _):
+        for i in range(PIECES * 4):
+            turned[k * PIECES * 4 + i] = tiles[k * PIECES * 4 + i].T
+        return 0
+
     def backward():
         def quad(g, _):
             base = mix(my_group, g, groups) * QUAD
@@ -189,10 +232,9 @@
                 for i in range(CHUNK // 2):
                     total = push[c, :, 2 * i * width : 2 * (i + 1) * width]
                     for h in range(QUAD // 2):
-                        total = total + lax.dot_general(
+                        total = total + jnp.dot(
                             pairs[h],
-                            weights(base, c, i, h),
-                            (((1,), (1,)), ((), ())),
+                            weights_turned(base, c, i, h),
                             preferred_element_type=jnp.float32,
                         )
                     push[c, :, 2 * i * width : 2 * (i + 1) * width] = total
@@ -217,36 +259,51 @@
 
         lax.fori_loop(0, chunks, block, 0)
 
+    def encode(load):
+        peak = jnp.max(jnp.abs(load), axis=0, keepdims=True)
+        power = jnp.ceil(jnp.log2(jnp.maximum(peak, 1e-30)))
+        level = jnp.floor(load * (LEVELS * jnp.exp2(-power)) + 0.5)
+        power = jnp.broadcast_to(power, (16, load.shape[1]))
+        rows = jnp.concatenate([level, power], axis=0)
+        return rows.astype(jnp.int32).astype(jnp.int16)
+
+    def decode(coded):
+        rows = coded.astype(jnp.int32).astype(jnp.float32)
+        return rows[:scen] * (jnp.exp2(rows[scen : scen + 1]) * (1.0 / LEVELS))
+
     def forward():
         def quad(g, _):
             base = mix(my_group, groups - 1 - g, groups) * QUAD
 
-            def chunk(c, _):
+            def chunk(c, totals):
+                done = []
                 for h in range(QUAD // 2):
-                    total = acc[h]
+                    total = totals[h]
                     for i in range(CHUNK // 2):
                         total = total + jnp.dot(
                             bar[c, :, 2 * i * width : 2 * (i + 1) * width],
                             weights(base, c, i, h),
                             preferred_element_type=jnp.float32,
                         )
-                    acc[h] = total
-                return 0
-
-            acc[...] = jnp.zeros(acc.shape, acc.dtype)
-            lax.fori_loop(0, chunks, chunk, 0)
-            for i in range(QUAD):
-                owner = base + i
-                load = acc[i // 2, :, (i % 2) * width : (i % 2 + 1) * width]
-
-                @pl.when(owner != me)
-                def _():
+                    done.append(total)
+                return tuple(done)
+
+            zero = jnp.zeros((scen, 2 * width), jnp.float32)
+            totals = (zero,) * (QUAD // 2)
+            if chunks == 1:
+                totals = chunk(0, totals)
+            else:
+                totals = lax.fori_loop(0, chunks, chunk, totals)
+            for h in range(QUAD // 2):
+                coded = encode(totals[h])
+                for q in range(2):
+                    owner = base + 2 * h + q
+                    load = coded[:, q * width : (q + 1) * width]
                     send_part[owner] = load
-                    remote(*part_ways, owner).start()
-
-                @pl.when(owner == me)
-                def _():
-                    recv_part[me] = load
+
+                    @pl.when(owner != me)
+                    def _():
+                        remote(*part_ways, owner).start()
 
             return 0
 
@@ -262,7 +319,7 @@
                     arrival(*part_ways, base + i).wait_recv()
 
             for i in range(QUAD):
-                part = recv_part[base + i]
+                part = decode(recv_part[base + i])
                 choice = recv_sel[base + i][0:1, :]
                 loads = tuple(
                     loads[b] + jnp.where(choice == b, part, 0.0) for b in range(link_here)
@@ -270,6 +327,7 @@
             return loads
 
         zero = jnp.zeros((scen, width), jnp.float32)
+        recv_part[me] = send_part[me]
         loads = lax.fori_loop(0, groups, add, (zero,) * link_here)
         for b in range(link_here):
             dual_out[b] = jnp.maximum(0.0, dual_out[b] + dual_step * (loads[b] - bound[b]))
@@ -281,7 +339,7 @@
             give(send_dual, peer, peer)
             remote(*dual_ways, peer).start()
 
-        peers(offer)
+        peers(offer, far_first=False)
         give(recv_dual, me, me)
 
         @pl.when(t == 0)
@@ -289,6 +347,7 @@
             for i in range(load_parts):
                 load_tiles(i).wait()
             load_flow.wait()
+            lax.fori_loop(0, tile_total // (PIECES * 4), turn, 0)
 
         backward()
         peers(lambda peer: arrival(*dual_ways, peer).wait_send())
@@ -310,22 +369,17 @@
     lax.fori_loop(0, ITERS + 1, phase, 0)
     save_flow.wait()
 
-    def finish(c, _):
-        for i in range(CHUNK):
-            b = c * CHUNK + i
-            flow[b] = cost_ref[pl.ds(b, 1), :] + push[c, :, i * width : (i + 1) * width]
-        part = pl.ds(c * CHUNK, CHUNK)
-        pltpu.make_async_copy(flow.at[part], rc_out.at[part], out_sem.at[c]).start()
-        return 0
-
-    lax.fori_loop(0, chunks, finish, 0)
-
-    def close(c, _):
-        part = pl.ds(c * CHUNK, CHUNK)
-        pltpu.make_async_copy(flow.at[part], rc_out.at[part], out_sem.at[c]).wait()
-        return 0
-
-    lax.fori_loop(0, chunks, close, 0)
+    share = blocks // PIECES
+    saves = []
+    for k in range(PIECES):
+        for b in range(k * share, (k + 1) * share):
+            i = b % CHUNK
+            flow[b] = cost_ref[b : b + 1, :] + push[b // CHUNK, :, i * width : (i + 1) * width]
+        part = pl.ds(k * share, share)
+        saves.append(pltpu.make_async_copy(flow.at[part], rc_out.at[part], out_sem.at[k]))
+        saves[-1].start()
+    for copy in saves:
+        copy.wait()
 
 
 def body(
@@ -361,9 +415,18 @@
             jax.ShapeDtypeStruct(flow_start.shape, jnp.float32),
             jax.ShapeDtypeStruct(flow_start.shape, jnp.float32),
         ),
-        in_specs=[pl.BlockSpec(memory_space=pltpu.SMEM)] + [vmem] * 6 + [anywhere] * 2,
+        in_specs=[anywhere] * 9,
         out_specs=(vmem, anywhere, anywhere),
         scratch_shapes=[
+            pltpu.SMEM(inv.shape, jnp.int32),
+            pltpu.VMEM(sel.shape, jnp.int32),
+            pltpu.VMEM(fail_links.shape, jnp.int32),
+            pltpu.VMEM(dual_start.shape, jnp.float32),
+            pltpu.VMEM(path_cost.shape, jnp.float32),
+            pltpu.VMEM(path_upper.shape, jnp.float32),
+            pltpu.VMEM(link_capacity.shape, jnp.float32),
+            dma((7,)),
+            pltpu.VMEM((tile_total + 1, width, width), jnp.bfloat16),
             pltpu.VMEM((tile_total + 1, width, width), jnp.bfloat16),
             pltpu.VMEM(flow_start.shape, jnp.float32),
             pltpu.VMEM((chunks, scen, CHUNK * width), jnp.float32),
@@ -371,13 +434,12 @@
             pltpu.VMEM(dual_start.shape, jnp.float32),
             pltpu.VMEM((devs, scen, width), jnp.bfloat16),
             pltpu.VMEM((devs, scen, width), jnp.bfloat16),
-            pltpu.VMEM((devs, scen, width), jnp.float32),
-            pltpu.VMEM((devs, scen, width), jnp.float32),
+            pltpu.VMEM((devs, scen + 16, width), jnp.int16),
+            pltpu.VMEM((devs, scen + 16, width), jnp.int16),
             pltpu.VMEM((devs, 8, width), jnp.int32),
-            pltpu.VMEM((QUAD // 2, scen, 2 * width), jnp.float32),
             dma((4,)),
             dma(()),
-            dma((chunks,)),
+            dma((PIECES,)),
             dma((devs,)),
             dma((devs,)),
             dma((devs,)),
@@ -386,7 +448,7 @@
             dma((devs,)),
         ],
         compiler_params=pltpu.CompilerParams(
-            collective_id=0, has_side_effects=True, vmem_limit_bytes=48 * 1024 * 1024
+            collective_id=0, has_side_effects=True, vmem_limit_bytes=60 * 1024 * 1024
         ),
     )(
         inv,

time: 86.3 us -> 68.5 us (0.79)
  Pallas kernels: 76.1 us -> 58.7 us
    pallas_call x1, Pallas kernels: 76.1 us -> 58.7 us  [body(): pl.pallas_call(functools.partial(kernel, devs), out_shape=(jax.ShapeDtype...]
    unnamed x15 -> x3, local copies, waits for them, and re-layouts: 7.51 us -> 6.09 us
where the time goes in v2:
time: 68.5 us; the launch traced here: 68.2 us
  Pallas kernels  58.7 us (86%)
  local copies, waits for them, and re-layouts  6.8 us (10%)
  other arithmetic  2 us (3%)
    pallas_call x1, Pallas kernels, body(): pl.pallas_call(functools.partial(kernel, devs), out_shape=(jax.ShapeDtype...  58.7 us
    unnamed x3, local copies, waits for them, and re-layouts  6.09 us

profile of v2, /device:TPU:0, one launch (start us, length us, event | category | flops | bytes accessed | tf_op | source)
XLA Modules:
  0.0 68.2 jit_solution(10236068293721512996)
XLA Ops:
  0.6 0.7 iota_compare_fusion.1
  1.3 0.7 %add_select_fusion.1 = (s32[32,9]{0,1:T(8,128)S(1)}, s32[32,9]{0,1:T(8,128)S(1)}, s32[32,9]{0,1:T(8,128)S(1)}) fusion(s32[32,9]{0,1:T(8,128)} %param.10), kind=kLoop, calls=%fused_computation.5 | loop fusion | flops 6048 | bytes 4608 | tf_op jit(solution)/shard_map/jit(floor_divide)/jit(_where)/select_n | solution.py:400
  2.0 0.6 select_reduce_fusion
  2.6 0.7 %broadcast_in_dim.36.sel_hbm = s32[16,8,128]{2,1,0:T(8,128)} broadcast(s32[16]{0:T(128)S(1)} %get-tuple-element.9), dimensions={0} | broadcast | bytes 65600 | tf_op jit(solution)/shard_map/broadcast_in_dim | solution.py:406
  3.3 58.7 %shard_map.112 = (f32[2,64,128]{2,1,0:T(8,128)}, f32[32,64,128]{2,1,0:T(8,128)}, f32[32,64,128]{2,1,0:T(8,128)}) custom-call(s32[16,32]{1,0:T(8,128)} %get-tuple-element.10.inv_hbm, s32[16,8,128]{2,1,0:T(8,128)} %broadcast_in_dim.36.sel_hbm, s32[64,128]{1,0:T(8,128)} %fail_hbm.1, f32[2,64,128]{2,1,0:T(8,128)} %dual_hbm.1, f32[32,128]{1,0:T(8,128)} %cost_hbm.1, ...), custom_call_target="tpu_custom_call" | custom-call | tf_op jit(solution)/shard_map/pallas_call | solution.py:411
  62.1 2.3 %copy.17 = f32[32,64,128]{2,1,0:T(8,128)} copy(f32[32,64,128]{2,1,0:T(8,128)} %get-tuple-element.17) | data formatting | bytes 2097152
  64.4 1.5 %copy.18 = f32[2,64,128]{2,1,0:T(8,128)} copy(f32[2,64,128]{2,1,0:T(8,128)} %get-tuple-element.18) | data formatting | bytes 131072
  65.9 2.3 %copy.19 = f32[32,64,128]{2,1,0:T(8,128)} copy(f32[32,64,128]{2,1,0:T(8,128)} %get-tuple-element.19) | data formatting | bytes 2097152

commit v3 on v2

--- a/solution.py
+++ b/solution.py
@@ -30,8 +30,8 @@
 
 def kernel(
     devs,
-    inv_hbm,
-    sel_hbm,
+    link_hbm,
+    count_hbm,
     fail_hbm,
     dual_hbm,
     cost_hbm,
@@ -43,24 +43,29 @@
     flow_out,
     rc_out,
     inv_ref,
-    sel_ref,
+    link_ref,
+    count_ref,
+    inv_vec,
+    sel_vec,
+    all_sel,
     fail_ref,
     dual_ref,
     cost_ref,
     upper_ref,
     cap_ref,
     small_sem,
+    inv_sem,
     tiles,
     turned,
     flow,
     push,
     bar,
     bound,
+    dual_now,
     send_dual,
     recv_dual,
     send_part,
     recv_part,
-    recv_sel,
     tile_sem,
     flow_sem,
     out_sem,
@@ -89,11 +94,11 @@
         pltpu.make_async_copy(src, dst, small_sem.at[i])
         for i, (src, dst) in enumerate(
             (
-                (sel_hbm, sel_ref),
+                (link_hbm, link_ref),
+                (count_hbm, count_ref),
                 (dual_hbm, dual_ref),
                 (fail_hbm, fail_ref),
                 (cap_hbm, cap_ref),
-                (inv_hbm, inv_ref),
                 (cost_hbm, cost_ref),
                 (upper_hbm, upper_ref),
             )
@@ -126,7 +131,16 @@
             device_id_type=pl.DeviceIdType.MESH,
         )
 
-    sel_ways = (sel_ref, recv_sel, sel_send, sel_recv)
+    def sel_way(peer, slot):
+        return pltpu.make_async_remote_copy(
+            src_ref=sel_vec,
+            dst_ref=all_sel.at[slot],
+            send_sem=sel_send.at[peer],
+            recv_sem=sel_recv.at[slot],
+            device_id={"path": peer},
+            device_id_type=pl.DeviceIdType.MESH,
+        )
+
     dual_ways = (send_dual, recv_dual, dual_send, dual_recv)
     part_ways = (send_part, recv_part, part_send, part_recv)
 
@@ -154,10 +168,28 @@
     peers(greet)
     for copy in small:
         copy.wait()
+
+    slots = link_ref.shape[0]
+    grid = (devs, blocks)
+    first_slot = lax.broadcasted_iota(jnp.int32, grid, 1) * slots
+    owner_link = lax.broadcasted_iota(jnp.int32, grid, 0) * link_here
+    count = jnp.broadcast_to(count_ref[...], grid)
+    place = jnp.full(grid, tile_total, jnp.int32)
+    wanted = jnp.zeros(grid, jnp.int32)
+    for k in range(slots):
+        offset = jnp.broadcast_to(link_ref[k : k + 1, :], grid) - owner_link
+        hit = (offset >= 0) & (offset < link_here) & (count > k)
+        place = jnp.where(hit, first_slot + k, place)
+        wanted = jnp.where(hit, offset, wanted)
+    inv_vec[...] = jnp.zeros(inv_vec.shape, jnp.int32)
+    inv_vec[:, :blocks] = place
+    load_inv = pltpu.make_async_copy(inv_vec, inv_ref, inv_sem)
+    load_inv.start()
+    sel_vec[...] = jnp.broadcast_to(jnp.max(wanted, axis=1, keepdims=True), sel_vec.shape)
+    all_sel[me] = sel_vec[...]
     pl.semaphore_wait(barrier, devs - 1)
 
-    peers(lambda peer: remote(*sel_ways, peer).start())
-    recv_sel[me] = sel_ref[me]
+    peers(lambda peer: sel_way(peer, me).start())
 
     tiles[tile_total] = jnp.zeros((width, width), tiles.dtype)
     turned[tile_total] = jnp.zeros((width, width), tiles.dtype)
@@ -180,16 +212,16 @@
         _, *alive = lax.fori_loop(0, width // 8, strike, (ids, *alive))
     for b in range(link_here):
         bound[b] = cap_ref[b : b + 1, :] * alive[b]
-        dual_out[b] = dual_ref[b]
-
-    peers(lambda peer: arrival(*sel_ways, peer).wait_recv(), far_first=False)
-    peers(lambda peer: arrival(*sel_ways, peer).wait_send())
+        dual_now[b] = dual_ref[b]
+
+    peers(lambda peer: sel_way(peer, peer).wait_recv(), far_first=False)
+    peers(lambda peer: sel_way(peer, peer).wait_send())
 
     def give(dst, index, peer):
-        choice = recv_sel[peer][0:1, :]
-        picked = dual_out[0]
+        choice = all_sel[peer, pl.ds(me, 1), :]
+        picked = dual_now[0]
         for b in range(1, link_here):
-            picked = jnp.where(choice == b, dual_out[b], picked)
+            picked = jnp.where(choice == b, dual_now[b], picked)
         dst[index] = picked.astype(jnp.bfloat16)
 
     def weights(base, c, i, h):
@@ -245,16 +277,17 @@
         push[...] = jnp.zeros(push.shape, push.dtype)
         lax.fori_loop(0, groups, quad, 0)
 
-    def primal():
+    def primal(t):
         def block(c, _):
             for i in range(CHUNK):
                 b = c * CHUNK + i
                 side = slice(i * width, (i + 1) * width)
                 now = flow[b]
                 price = cost_ref[pl.ds(b, 1), :] + push[c, :, side]
-                new = jnp.clip(now - primal_step * price, 0.0, upper_ref[pl.ds(b, 1), :])
+                raw = now - primal_step * price
+                new = jnp.clip(raw, 0.0, upper_ref[pl.ds(b, 1), :])
                 bar[c, :, side] = (2.0 * new - now).astype(jnp.bfloat16)
-                flow[b] = new
+                flow[b] = jnp.where(t == ITERS - 1, raw, new)
             return 0
 
         lax.fori_loop(0, chunks, block, 0)
@@ -320,7 +353,7 @@
 
             for i in range(QUAD):
                 part = decode(recv_part[base + i])
-                choice = recv_sel[base + i][0:1, :]
+                choice = all_sel[base + i, pl.ds(me, 1), :]
                 loads = tuple(
                     loads[b] + jnp.where(choice == b, part, 0.0) for b in range(link_here)
                 )
@@ -330,7 +363,9 @@
         recv_part[me] = send_part[me]
         loads = lax.fori_loop(0, groups, add, (zero,) * link_here)
         for b in range(link_here):
-            dual_out[b] = jnp.maximum(0.0, dual_out[b] + dual_step * (loads[b] - bound[b]))
+            raw = dual_now[b] + dual_step * (loads[b] - bound[b])
+            dual_out[b] = raw
+            dual_now[b] = jnp.maximum(0.0, raw)
 
     save_flow = pltpu.make_async_copy(flow, flow_out, flow_sem)
 
@@ -347,6 +382,7 @@
             for i in range(load_parts):
                 load_tiles(i).wait()
             load_flow.wait()
+            load_inv.wait()
             lax.fori_loop(0, tile_total // (PIECES * 4), turn, 0)
 
         backward()
@@ -354,7 +390,7 @@
 
         @pl.when(t < ITERS)
         def _():
-            primal()
+            primal(t)
 
             @pl.when(t == ITERS - 1)
             def _():
@@ -374,7 +410,7 @@
     for k in range(PIECES):
         for b in range(k * share, (k + 1) * share):
             i = b % CHUNK
-            flow[b] = cost_ref[b : b + 1, :] + push[b // CHUNK, :, i * width : (i + 1) * width]
+            flow[b] = push[b // CHUNK, :, i * width : (i + 1) * width]
         part = pl.ds(k * share, share)
         saves.append(pltpu.make_async_copy(flow.at[part], rc_out.at[part], out_sem.at[k]))
         saves[-1].start()
@@ -397,46 +433,45 @@
     blocks, slots, width, _ = tile_values.shape
     link_here, scen, _ = dual_start.shape
     tile_total = blocks * slots
-    owner_of = link_of_tile // link_here
-    used = jnp.arange(slots, dtype=jnp.int32)[None, :] < tile_count[:, None]
-    hits = (owner_of[None] == jnp.arange(devs, dtype=jnp.int32)[:, None, None]) & used[None]
-    place = jnp.arange(tile_total, dtype=jnp.int32).reshape(1, blocks, slots)
-    inv = jnp.min(jnp.where(hits, place, tile_total), axis=2)
-    sel = jnp.max(jnp.where(hits, (link_of_tile % link_here)[None], 0), axis=(1, 2))
-    sel = jnp.broadcast_to(sel[:, None, None], (devs, 8, width))
+    lanes = -(-blocks // 128) * 128
     chunks = blocks // CHUNK
     vmem = pl.BlockSpec(memory_space=pltpu.VMEM)
     anywhere = pl.BlockSpec(memory_space=pl.ANY)
     dma = pltpu.SemaphoreType.DMA
-    dual_final, flow_final, reduced = pl.pallas_call(
+    dual_raw, flow_raw, pushed = pl.pallas_call(
         functools.partial(kernel, devs),
         out_shape=(
             jax.ShapeDtypeStruct(dual_start.shape, jnp.float32),
             jax.ShapeDtypeStruct(flow_start.shape, jnp.float32),
             jax.ShapeDtypeStruct(flow_start.shape, jnp.float32),
         ),
-        in_specs=[anywhere] * 9,
+        in_specs=[pl.BlockSpec(memory_space=pltpu.HBM)] * 9,
         out_specs=(vmem, anywhere, anywhere),
         scratch_shapes=[
-            pltpu.SMEM(inv.shape, jnp.int32),
-            pltpu.VMEM(sel.shape, jnp.int32),
+            pltpu.SMEM((devs, lanes), jnp.int32),
+            pltpu.VMEM((slots, blocks), jnp.int32),
+            pltpu.VMEM((1, blocks), jnp.int32),
+            pltpu.VMEM((devs, lanes), jnp.int32),
+            pltpu.VMEM((devs, width), jnp.int32),
+            pltpu.VMEM((devs, devs, width), jnp.int32),
             pltpu.VMEM(fail_links.shape, jnp.int32),
             pltpu.VMEM(dual_start.shape, jnp.float32),
             pltpu.VMEM(path_cost.shape, jnp.float32),
             pltpu.VMEM(path_upper.shape, jnp.float32),
             pltpu.VMEM(link_capacity.shape, jnp.float32),
             dma((7,)),
+            dma(()),
             pltpu.VMEM((tile_total + 1, width, width), jnp.bfloat16),
             pltpu.VMEM((tile_total + 1, width, width), jnp.bfloat16),
             pltpu.VMEM(flow_start.shape, jnp.float32),
             pltpu.VMEM((chunks, scen, CHUNK * width), jnp.float32),
             pltpu.VMEM((chunks, scen, CHUNK * width), jnp.bfloat16),
             pltpu.VMEM(dual_start.shape, jnp.float32),
+            pltpu.VMEM(dual_start.shape, jnp.float32),
             pltpu.VMEM((devs, scen, width), jnp.bfloat16),
             pltpu.VMEM((devs, scen, width), jnp.bfloat16),
             pltpu.VMEM((devs, scen + 16, width), jnp.int16),
             pltpu.VMEM((devs, scen + 16, width), jnp.int16),
-            pltpu.VMEM((devs, 8, width), jnp.int32),
             dma((4,)),
             dma(()),
             dma((PIECES,)),
@@ -451,8 +486,8 @@
             collective_id=0, has_side_effects=True, vmem_limit_bytes=60 * 1024 * 1024
         ),
     )(
-        inv,
-        sel,
+        link_of_tile.T,
+        tile_count.reshape(1, blocks),
         fail_links,
         dual_start,
         path_cost,
@@ -461,7 +496,8 @@
         tile_values.reshape(tile_total, width, width),
         flow_start,
     )
-    return flow_final, dual_final, reduced
+    flow_final = jnp.clip(flow_raw, 0.0, path_upper[:, None, :])
+    return flow_final, jnp.maximum(0.0, dual_raw), path_cost[:, None, :] + pushed
 
 
 def solution(mesh):

time: 68.5 us -> 66.1 us (0.965)
  local copies, waits for them, and re-layouts: 6.8 us -> 0.01 us
  other arithmetic: 2 us -> 4.78 us
  Pallas kernels: 58.7 us -> 60.5 us
    unnamed x3 -> x4, local copies, waits for them, and re-layouts: 6.09 us -> 0.01 us
    min x0 -> x1, other arithmetic: none -> 3.31 us  [body(): flow_final = jnp.clip(flow_raw, 0.0, path_upper[:, None, :])]
    pallas_call x1, Pallas kernels: 58.7 us -> 60.5 us  [body(): pl.pallas_call(functools.partial(kernel, devs), out_shape=(jax.ShapeDtype...]
    max x0 -> x1, other arithmetic: none -> 1.47 us  [body(): jnp.maximum(0.0, dual_raw)]
    broadcast_in_dim x1 -> x0, local copies, waits for them, and re-layouts: 0.71 us -> none  [body(): sel = jnp.broadcast_to(sel[:, None, None], (devs, 8, width))]
    select_n x1 -> x0, other arithmetic: 0.71 us -> none  [body(): owner_of = link_of_tile // link_here]
where the time goes in v3:
time: 66.1 us; the launch traced here: 66 us
  Pallas kernels  60.5 us (92%)
  other arithmetic  4.78 us (7%)
  between operations  0.67 us (1%)
    pallas_call x1, Pallas kernels, body(): pl.pallas_call(functools.partial(kernel, devs), out_shape=(jax.ShapeDtype...  60.5 us
    min x1, other arithmetic, body(): flow_final = jnp.clip(flow_raw, 0.0, path_upper[:, None, :])  3.31 us
    max x1, other arithmetic, body(): jnp.maximum(0.0, dual_raw)  1.47 us

profile of v3, /device:TPU:0, one launch (start us, length us, event | category | flops | bytes accessed | tf_op | source)
XLA Modules:
  0.0 66.0 jit_solution(4889383549754622348)
XLA Ops:
  0.6 0.0 copy-start.1
  0.6 0.0 copy-start
  0.7 60.5 %shard_map.112 = (f32[2,64,128]{2,1,0:T(8,128)}, f32[32,64,128]{2,1,0:T(8,128)}, f32[32,64,128]{2,1,0:T(8,128)}) custom-call(s32[9,32]{1,0:T(8,128)} %bitcast.4, s32[1,32]{1,0:T(1,128)} %bitcast.5, s32[64,128]{1,0:T(8,128)} %fail_hbm.1, f32[2,64,128]{2,1,0:T(8,128)} %dual_hbm.1, f32[32,128]{1,0:T(8,128)} %cost_hbm.1, f32[32,128]{1,0:T(8,128)} %upper_hbm.1, ...), custom_call_target="tpu_custom_call" | custom-call | tf_op jit(solution)/shard_map/pallas_call | solution.py:441
  61.1 0.0 copy-done.1
  61.2 0.0 copy-done
  61.2 3.3 %maximum_minimum_fusion = (f32[32,64,128]{2,1,0:T(8,128)}, f32[32,64,128]{2,1,0:T(8,128)}) fusion(f32[32,64,128]{2,1,0:T(8,128)} %get-tuple-element.6, f32[32,128]{1,0:T(8,128)S(1)} %copy-done.1, f32[32,64,128]{2,1,0:T(8,128)} %get-tuple-element.8, f32[32,128]{1,0:T(8,128)S(1)} %copy-done), kind=kLoop, calls=%fused_computation | loop fusion | flops 786432 | bytes 4227072 | tf_op jit(solution)/shard_map/jit(clip)/min | solution.py:499
  64.5 1.5 %broadcast_maximum_fusion = f32[2,64,128]{2,1,0:T(8,128)} fusion(f32[2,64,128]{2,1,0:T(8,128)} %get-tuple-element.7), kind=kLoop, calls=%fused_computation.2 | loop fusion | flops 16384 | bytes 131072 | tf_op jit(solution)/shard_map/max | solution.py:500
Async XLA Ops:
  0.6 60.5 %copy-start.1 = (f32[32,128]{1,0:T(8,128)S(1)}, f32[32,128]{1,0:T(8,128)}, u32[]{:S(2)}) copy-start(f32[32,128]{1,0:T(8,128)} %upper_hbm.1) | copy-start | bytes 49156
  0.6 60.5 %copy-start = (f32[32,128]{1,0:T(8,128)S(1)}, f32[32,128]{1,0:T(8,128)}, u32[]{:S(2)}) copy-start(f32[32,128]{1,0:T(8,128)} %cost_hbm.1) | copy-start | bytes 49156

commit v4 on v3

--- a/solution.py
+++ b/solution.py
@@ -215,7 +215,6 @@
         dual_now[b] = dual_ref[b]
 
     peers(lambda peer: sel_way(peer, peer).wait_recv(), far_first=False)
-    peers(lambda peer: sel_way(peer, peer).wait_send())
 
     def give(dst, index, peer):
         choice = all_sel[peer, pl.ds(me, 1), :]
@@ -377,8 +376,13 @@
         peers(offer, far_first=False)
         give(recv_dual, me, me)
 
+        @pl.when(t > 0)
+        def _():
+            peers(lambda peer: arrival(*part_ways, peer).wait_send())
+
         @pl.when(t == 0)
         def _():
+            peers(lambda peer: sel_way(peer, peer).wait_send())
             for i in range(load_parts):
                 load_tiles(i).wait()
             load_flow.wait()
@@ -386,7 +390,6 @@
             lax.fori_loop(0, tile_total // (PIECES * 4), turn, 0)
 
         backward()
-        peers(lambda peer: arrival(*dual_ways, peer).wait_send())
 
         @pl.when(t < ITERS)
         def _():
@@ -397,8 +400,12 @@
                 save_flow.start()
 
             forward()
+            peers(lambda peer: arrival(*dual_ways, peer).wait_send())
             dual_step_all()
-            peers(lambda peer: arrival(*part_ways, peer).wait_send())
+
+        @pl.when(t == ITERS)
+        def _():
+            peers(lambda peer: arrival(*dual_ways, peer).wait_send())
 
         return 0
 

time: 66.1 us -> 65.6 us (level)
  no operation moved by 1% of the time
where the time goes in v4:
time: 65.6 us; the launch traced here: 65.4 us
  Pallas kernels  60 us (91%)
  other arithmetic  4.78 us (7%)
  between operations  0.67 us (1%)
    pallas_call x1, Pallas kernels, body(): pl.pallas_call(functools.partial(kernel, devs), out_shape=(jax.ShapeDtype...  60 us
    min x1, other arithmetic, body(): flow_final = jnp.clip(flow_raw, 0.0, path_upper[:, None, :])  3.31 us
    max x1, other arithmetic, body(): jnp.maximum(0.0, dual_raw)  1.47 us

profile of v4, /device:TPU:0, one launch (start us, length us, event | category | flops | bytes accessed | tf_op | source)
XLA Modules:
  0.0 65.4 jit_solution(6662006461912883646)
XLA Ops:
  0.6 0.0 copy-start.1
  0.6 0.0 copy-start
  0.7 60.0 %shard_map.112 = (f32[2,64,128]{2,1,0:T(8,128)}, f32[32,64,128]{2,1,0:T(8,128)}, f32[32,64,128]{2,1,0:T(8,128)}) custom-call(s32[9,32]{1,0:T(8,128)} %bitcast.4, s32[1,32]{1,0:T(1,128)} %bitcast.5, s32[64,128]{1,0:T(8,128)} %fail_hbm.1, f32[2,64,128]{2,1,0:T(8,128)} %dual_hbm.1, f32[32,128]{1,0:T(8,128)} %cost_hbm.1, f32[32,128]{1,0:T(8,128)} %upper_hbm.1, ...), custom_call_target="tpu_custom_call" | custom-call | tf_op jit(solution)/shard_map/pallas_call | solution.py:448
  60.6 0.0 copy-done.1
  60.6 0.0 copy-done
  60.6 3.3 %maximum_minimum_fusion = (f32[32,64,128]{2,1,0:T(8,128)}, f32[32,64,128]{2,1,0:T(8,128)}) fusion(f32[32,64,128]{2,1,0:T(8,128)} %get-tuple-element.6, f32[32,128]{1,0:T(8,128)S(1)} %copy-done.1, f32[32,64,128]{2,1,0:T(8,128)} %get-tuple-element.8, f32[32,128]{1,0:T(8,128)S(1)} %copy-done), kind=kLoop, calls=%fused_computation | loop fusion | flops 786432 | bytes 4227072 | tf_op jit(solution)/shard_map/jit(clip)/min | solution.py:506
  64.0 1.5 %broadcast_maximum_fusion = f32[2,64,128]{2,1,0:T(8,128)} fusion(f32[2,64,128]{2,1,0:T(8,128)} %get-tuple-element.7), kind=kLoop, calls=%fused_computation.2 | loop fusion | flops 16384 | bytes 131072 | tf_op jit(solution)/shard_map/max | solution.py:507
Async XLA Ops:
  0.6 60.0 %copy-start.1 = (f32[32,128]{1,0:T(8,128)S(1)}, f32[32,128]{1,0:T(8,128)}, u32[]{:S(2)}) copy-start(f32[32,128]{1,0:T(8,128)} %upper_hbm.1) | copy-start | bytes 49156
  0.6 60.0 %copy-start = (f32[32,128]{1,0:T(8,128)S(1)}, f32[32,128]{1,0:T(8,128)}, u32[]{:S(2)}) copy-start(f32[32,128]{1,0:T(8,128)} %cost_hbm.1) | copy-start | bytes 49156
